TPU v7x, 256 devices: a whole 4x4x8 slice. The times are simulated.
256 devices in a mesh: replica: 32 (over z_hi, y, core), shard: 8 (over x, z_lo).
Axes of the slice: x: 4, y: 4, z: 8 (z_hi: 4, z_lo: 2; z = z_hi * 2 + z_lo), core: 2. Of those that a mesh axis runs over, the one named last changes fastest.
Arguments:
- weight: bfloat16 [256, 8192], P(None, 'shard'), may hold values from -6 to 6
- momentum: float32 [32, 256, 8192], P('replica', None, 'shard'), may hold values from -6 to 6
- grad: bfloat16 [32, 256, 8192], P('replica', None, 'shard'), may hold values from -6 to 6
- positions: int32 [32, 4, 128, 32], P('replica', None, 'shard'), may hold values from 0 to 4095, as said below
Outputs:
- kept_state: float32 [32, 256, 8192], P('replica', None, 'shard')
- direction: bfloat16 [256, 8192], P(None, 'shard')
- new_weight: bfloat16 [256, 8192], replicated
Inputs may be any that keep to these rules, and one draw needn't show every extreme that they name: The 32 positions of one block on one replica are distinct; replicas choose independently.
All inputs are finite; a program needn't handle non-finite values.
Results may differ from a plain program's by a relative error of at most 0.001.
Values may be sent and summed in bfloat16 or wider, within the bound.
No kernel may reach another device: no remote copies, remote signals or barrier semaphores. Data moves between devices by JAX's collectives and lax.ppermute only.
A program may use at most 64 MiB of HBM per device.

v0:
```python
import math
import jax
import jax.numpy as jnp
from jax import lax
from jax.sharding import Mesh
from jax.sharding import PartitionSpec as P

GROUP = 64
REPLICA = ("replica_0", "replica_1", "replica_2")
beta_decay = 0.9
step_rate = 0.02


def padded_to(lines, size):
    spare = -len(lines) % size
    return jnp.pad(lines, [(0, spare)] + [(0, 0)] * (lines.ndim - 1))


def copy_for_each(array, axis):
    copies = jnp.broadcast_to(array, (lax.axis_size(axis), *array.shape))
    return lax.all_to_all(copies, axis, split_axis=0, concat_axis=0, tiled=True)


def laid_out(blocks, dim):
    blocks = jnp.moveaxis(blocks, 0, dim)
    shape = blocks.shape
    return blocks.reshape(*shape[:dim], shape[dim] * shape[dim + 1], *shape[dim + 2 :])


def whole_of(array, axes, dim):
    far, near = axes
    blocks = copy_for_each(copy_for_each(array, far), near)
    return laid_out(blocks.swapaxes(0, 1).reshape(-1, *array.shape), dim)


def in_blocks(array, dim, size):
    before, after = (array.shape[:dim], array.shape[dim + 1 :])
    return jnp.moveaxis(array.reshape(*before, size, -1, *after), dim, 0)


def sent_and_summed(array, axis, dim):
    size = lax.axis_size(axis)
    blocks = lax.all_to_all(in_blocks(array, dim, size), axis, 0, 0, tiled=True)
    return jnp.sum(blocks, axis=0)


def sum_in_two_steps(array, axes, dim):
    far, near = axes
    blocks = in_blocks(array, dim, lax.axis_size(far))
    nearer = sent_and_summed(blocks, near, dim + 1)
    arrived = lax.all_to_all(nearer, far, split_axis=0, concat_axis=0, tiled=True)
    return arrived.sum(axis=0)


def sum_by_parts(array, axes):
    lines = array.reshape(-1, array.shape[-1])
    padded = padded_to(lines, lax.axis_size(axes[0]) * lax.axis_size(axes[1]))
    whole = whole_of(sum_in_two_steps(padded, axes, 0), axes, 0)
    return lax.slice_in_dim(whole, 0, len(lines)).reshape(array.shape)


def dct_basis():
    freq = jnp.arange(GROUP, dtype=jnp.float32)[:, None]
    cells = jnp.arange(GROUP, dtype=jnp.float32)[None, :]
    scales = jnp.where(freq == 0, math.sqrt(1.0 / GROUP), math.sqrt(2.0 / GROUP))
    return scales * jnp.cos(math.pi * (2.0 * cells + 1.0) * freq / (2.0 * GROUP))


def basis_rows(index, basis_table):
    one_hot = (index[..., None] == jnp.arange(GROUP, dtype=jnp.int32)).astype(jnp.float32)
    return jnp.einsum("xyka,ai->xyki", one_hot, basis_table, precision=lax.Precision.HIGHEST)


def extract(field, pos_table, basis_table):
    row_blocks, col_blocks = (pos_table.shape[0], pos_table.shape[1])
    left_rows = basis_rows(pos_table // GROUP, basis_table)
    right_rows = basis_rows(pos_table % GROUP, basis_table)
    block_view = field.reshape(row_blocks, GROUP, col_blocks, GROUP)
    inner_prod = jnp.einsum(
        "xyki,xiyj->xykj", left_rows, block_view, precision=lax.Precision.HIGHEST
    )
    return jnp.sum(inner_prod * right_rows, axis=-1)


def expand(values, pos_table, basis_table):
    row_blocks, col_blocks = (pos_table.shape[0], pos_table.shape[1])
    left_rows = basis_rows(pos_table // GROUP, basis_table)
    right_rows = basis_rows(pos_table % GROUP, basis_table)
    dense = jnp.einsum(
        "xyki,xyk,xykj->xiyj", left_rows, values, right_rows, precision=lax.Precision.HIGHEST
    )
    return dense.reshape(row_blocks * GROUP, col_blocks * GROUP)


def fill_grid(values, pos_table):
    row_blocks, col_blocks = (pos_table.shape[0], pos_table.shape[1])
    row_index = jnp.arange(row_blocks, dtype=jnp.int32)[:, None, None]
    col_index = jnp.arange(col_blocks, dtype=jnp.int32)[None, :, None]
    flat = jnp.zeros((row_blocks, col_blocks, GROUP * GROUP), jnp.float32)
    return flat.at[row_index, col_index, pos_table].add(values)


def decode(grid, basis_table):
    row_blocks, col_blocks = (grid.shape[0], grid.shape[1])
    square = grid.reshape(row_blocks, col_blocks, GROUP, GROUP)
    dense = jnp.einsum(
        "ai,xyab,bj->xiyj", basis_table, square, basis_table, precision=lax.Precision.HIGHEST
    )
    return dense.reshape(row_blocks * GROUP, col_blocks * GROUP)


def per_device(weight, momentum, grad, positions):
    basis_table = dct_basis()
    own_pos = positions[0]
    moved = beta_decay * momentum[0] + grad[0].astype(jnp.float32)
    picked = extract(moved, own_pos, basis_table)
    kept_state = moved - expand(picked, own_pos, basis_table)
    summed = sum_by_parts(fill_grid(picked, own_pos), (("replica_0", "replica_1"), "replica_2"))
    smooth = jnp.tanh(decode(summed, basis_table))
    updated = (weight.astype(jnp.float32) - step_rate * smooth).astype(jnp.bfloat16)
    new_weight = lax.all_gather(updated, "shard", axis=1, tiled=True)
    direction = smooth.astype(jnp.bfloat16)
    return (kept_state[None], direction, new_weight)


def solution(mesh):
    split = Mesh(
        mesh.devices.reshape(4, 4, 2, mesh.shape["shard"]),
        ("replica_0", "replica_1", "replica_2", "shard"),
    )
    in_specs = (
        P(None, "shard"),
        P(REPLICA, None, "shard"),
        P(REPLICA, None, "shard"),
        P(REPLICA, None, "shard", None),
    )
    out_specs = (P(REPLICA, None, "shard"), P(None, "shard"), P())
    return jax.shard_map(
        per_device, mesh=split, in_specs=in_specs, out_specs=out_specs, check_vma=False
    )
```

profile of v0, /device:TPU:1, one launch (start us, length us, event | category | flops | bytes accessed | tf_op | source)
XLA Modules:
  0.0 219.3 jit_solution(12417028372073017833)
XLA Ops:
  7.2 0.0 all-gather.2.cloned.1.call-start
  7.2 0.0 copy-start.1
  7.2 0.0 copy-start.2
  7.2 0.9 add_select_fusion
  8.2 0.8 compare_select_fusion
  8.9 0.8 fusion.10
  9.7 0.8 fusion.11
  10.5 0.0 copy-done.1
  10.5 0.0 copy-done.2
  10.5 0.1 convert_add_fusion
  10.7 0.0 copy-start.3
  10.7 0.0 copy-start.4
  10.7 1.9 add.62
  12.6 0.0 copy-done.3
  12.6 0.1 and_reduce_fusion
  12.7 0.0 copy-done.4
  12.7 0.1 multiply_reduce_fusion
  12.8 0.1 reshape.127
  12.8 4.2 %fusion.5 = f32[4,16,32]{2,1,0:T(8,128)S(1)} fusion(f32[4,16,32,64]{3,2,1,0:T(8,128)S(1)} %fusion.11, f32[4,16,32,64]{3,2,1,0:T(8,128)S(1)} %fusion.10, f32[4,64,16,64]{3,2,1,0:T(8,128)} %add.62), kind=kOutput, calls=%fused_computation.7 | convolution fusion | flops 100923392 | bytes 2105344 | tf_op jit(solution)/shard_map/xyki,xiyj->xykj/dot_general | solution.py:79
  17.0 0.1 reshape.129
  17.1 12.2 %scatter_custom_fusion = f32[262144]{0:T(1024)} fusion(s32[2048]{0:T(1024)S(1)} %reshape.127, f32[2048]{0:T(1024)S(1)} %reshape.129, f32[]{:T(128)} %constant.54.clone.1), kind=kCustom, calls=%fused_computation.16 | custom fusion | flops 2048 | bytes 1048580
  29.3 2.7 %reshape_reshape.3 = f32[16,2,2,4096]{3,2,1,0:T(2,128)} reshape(f32[262144]{0:T(1024)} %scatter_custom_fusion) | data formatting | bytes 2097152 | tf_op jit(solution)/shard_map/reshape;reshape | solution.py:38
  32.1 1.3 copy.37
  33.4 8.2 %all_to_all.20 = f32[2,16,2,4096]{3,2,1,0:T(2,128)} all-to-all(f32[2,16,2,4096]{3,2,1,0:T(2,128)S(1)} %copy.37), channel_id=1, replica_groups=mesh['replica_0'=4,'replica_1'=4,'replica_2'=2,'shard'=8] {'replica_2'}, dimensions={0} | all-to-all | bytes 2097152 | tf_op jit(solution)/shard_map/all_to_all | solution.py:43
  41.6 2.9 %reduce_sum.28 = f32[16,2,4096]{2,1,0:T(2,128)} reduce(f32[2,16,2,4096]{3,2,1,0:T(2,128)} %all_to_all.20, f32[]{:T(128)} %constant.54.clone.1), dimensions={0}, to_apply=%region_2.3 | reduce | flops 131072 | bytes 1572868 | tf_op jit(solution)/shard_map/reduce_sum | solution.py:44
  44.5 24.6 %all_to_all.21 = f32[16,2,4096]{2,1,0:T(2,128)} all-to-all(f32[16,2,4096]{2,1,0:T(2,128)} %reduce_sum.28), channel_id=1, replica_groups=mesh['replica_0'=4,'replica_1'=4,'replica_2'=2,'shard'=8] {'replica_0','..., dimensions={0} | all-to-all | bytes 1048576 | tf_op jit(solution)/shard_map/all_to_all | solution.py:51
  69.1 1.2 reduce_sum.29
  70.3 0.2 broadcast_in_dim.23
  70.5 20.8 %all_to_all.22 = f32[16,2,4096]{2,1,0:T(2,128)S(1)} all-to-all(f32[16,2,4096]{2,1,0:T(2,128)S(1)} %broadcast_in_dim.23), channel_id=1, replica_groups=mesh['replica_0'=4,'replica_1'=4,'replica_2'=2,'shard'=8] {'replica_0','..., dimensions={0} | all-to-all | bytes 1048576 | tf_op jit(solution)/shard_map/all_to_all | solution.py:21
  91.3 0.6 broadcast_in_dim.24
  91.9 7.8 %all_to_all.23 = f32[2,16,2,4096]{3,2,1,0:T(2,128)S(1)} all-to-all(f32[2,16,2,4096]{3,2,1,0:T(2,128)S(1)} %broadcast_in_dim.24), channel_id=1, replica_groups=mesh['replica_0'=4,'replica_1'=4,'replica_2'=2,'shard'=8] {'replica_2'}, dimensions={0} | all-to-all | bytes 2097152 | tf_op jit(solution)/shard_map/all_to_all | solution.py:21
  99.7 1.0 copy.39
  100.8 3.2 %reshape_reshape_reshape_reshape.3 = f32[4,16,64,64]{3,2,1,0:T(8,128)} reshape(f32[16,2,2,4096]{3,2,1,0:T(2,128)} %copy.39) | data formatting | bytes 2097152 | tf_op jit(solution)/shard_map/reshape;reshape;reshape;reshape | solution.py:105
  103.9 3.6 %fusion.19 = f32[4,16,64,64]{2,3,1,0:T(8,128)S(1)} fusion(f32[4,16,64,64]{3,2,1,0:T(8,128)} %reshape_reshape_reshape_reshape.3, f32[64]{0:T(128)S(1)} %get-tuple-element.8, f32[64]{0:T(128)S(1)} %get-tuple-element.7), kind=kOutput, calls=%fused_computation.32 | convolution fusion | flops 201338880 | bytes 2097664 | tf_op jit(solution)/shard_map/ai,xyab,bj->xiyj/dot_general | solution.py:106
  107.6 3.0 %multiply_bitcast_fusion = (f32[4,64,16,64]{3,1,2,0:T(8,128)S(1)}, bf16[4,64,16,64]{3,1,2,0:T(8,128)(2,1)}) fusion(f32[4,16,64,64]{2,3,1,0:T(8,128)S(1)} %fusion.19, f32[64]{0:T(128)S(1)} %get-tuple-element.8, f32[64]{0:T(128)S(1)} %get-tuple-element.7), kind=kOutput, calls=%fused_computation.3 | convolution fusion | flops 201863168 | bytes 2621952 | tf_op jit(solution)/shard_map/ai,xyab,bj->xiyj/dot_general | solution.py:106
  110.5 2.5 %copy.43 = f32[4,64,16,64]{3,2,1,0:T(8,128)} copy(f32[4,64,16,64]{3,1,2,0:T(8,128)S(1)} %get-tuple-element.3) | data formatting | bytes 2097152 | tf_op jit(solution)/shard_map/mul | solution.py:120
  113.1 2.7 %mul.124 = f32[256,1024]{1,0:T(8,128)} reshape(f32[4,64,16,64]{3,2,1,0:T(8,128)} %copy.43) | data formatting | bytes 2097152 | tf_op jit(solution)/shard_map/mul | solution.py:120
  115.8 2.3 %subtract_convert_fusion = bf16[256,1024]{1,0:T(8,128)(2,1)} fusion(f32[256,1024]{1,0:T(8,128)} %mul.124, bf16[256,1024]{1,0:T(8,128)(2,1)} %param.4), kind=kLoop, calls=%fused_computation.9 | loop fusion | flops 786432 | bytes 2097152 | tf_op jit(solution)/shard_map/convert_element_type | solution.py:120
  118.1 0.0 all-gather.2.cloned.1.call-update
  118.2 5.1 %convolution_bitcast_fusion = f32[4,64,16,64]{1,3,2,0:T(8,128)} fusion(f32[4,16,32,64]{3,2,1,0:T(8,128)S(1)} %fusion.10, f32[4,16,32,64]{3,2,1,0:T(8,128)S(1)} %fusion.11, f32[4,16,32]{2,1,0:T(8,128)S(1)} %fusion.5), kind=kOutput, calls=%fused_computation.5 | convolution fusion | flops 100794368 | bytes 2105344 | tf_op jit(solution)/shard_map/xyki,xyk,xykj->xiyj/dot_general | solution.py:89
  123.2 2.5 %copy.36 = f32[4,64,16,64]{3,2,1,0:T(8,128)S(1)} copy(f32[4,64,16,64]{1,3,2,0:T(8,128)} %convolution_bitcast_fusion) | data formatting | bytes 2097152 | tf_op jit(solution)/shard_map/xyki,xyk,xykj->xiyj/transpose | solution.py:89
  125.7 1.5 reshape.121
  127.3 0.0 copy-start
  127.3 2.5 %sub.16 = f32[1,256,1024]{2,1,0:T(8,128)} subtract(f32[1,256,1024]{2,1,0:T(8,128)S(1)} %convert_add_fusion, f32[1,256,1024]{2,1,0:T(8,128)} %reshape.121) | non-fusion elementwise | flops 262144 | bytes 3145728 | tf_op jit(solution)/shard_map/sub | solution.py:117
  129.7 0.0 copy-done
  129.7 0.7 copy.42
  130.4 1.5 convert_element_type.28
  131.9 75.9 %all-gather.2.cloned.1.call-done = bf16[256,8192]{1,0:T(8,128)(2,1)} async-done(((bf16[256,1024]{1,0:T(8,128)(2,1)}), bf16[256,8192]{1,0:T(8,128)(2,1)}) %all-gather.2.cloned.1.call-update) | async-done | bytes 4194320 | tf_op jit(solution)/shard_map/all_gather | solution.py:121
  207.9 4.6 %copy.55 = bf16[256,8192]{1,0:T(8,128)(2,1)} copy(bf16[256,8192]{1,0:T(8,128)(2,1)} %all-gather.2.cloned.1.call-done) | data formatting | bytes 8388608
  (4 shorter events, 0.0 us)
Async XLA Ops:
  7.2 200.7 %all-gather.2.cloned.1.call-start = ((), (), s32[]{:S(2)}) async-start(), calls=%async_computation.4 | async-start | bytes 4718592 | tf_op jit(solution)/shard_map/all_gather | solution.py:121
  7.2 3.3 %copy-start.1 = (f32[1,256,1024]{2,1,0:T(8,128)S(1)}, f32[1,256,1024]{2,1,0:T(8,128)}, u32[]{:S(2)}) copy-start(f32[1,256,1024]{2,1,0:T(8,128)} %param.5) | copy-start | bytes 3145732
  7.2 3.3 %copy-start.2 = (bf16[1,256,1024]{2,1,0:T(8,128)(2,1)S(1)}, bf16[1,256,1024]{2,1,0:T(8,128)(2,1)}, u32[]{:S(2)}) copy-start(bf16[1,256,1024]{2,1,0:T(8,128)(2,1)} %param.6) | copy-start | bytes 1572868
  10.7 1.9 copy-start.3
  10.7 2.0 copy-start.4
  127.3 2.5 %copy-start = (bf16[4,64,16,64]{3,1,2,0:T(8,128)(2,1)S(1)}, bf16[4,64,16,64]{3,1,2,0:T(8,128)(2,1)}, u32[]{:S(2)}) copy-start(bf16[4,64,16,64]{3,1,2,0:T(8,128)(2,1)} %get-tuple-element.4) | copy-start | bytes 1572868
Sparse Core Ops, SparseCore 0:
  118.3 89.5 all-gather.1
where the time goes:
time: 220 us; the launch traced here: 219 us
  waiting for transfers between devices  76 us (35%)
  blocking collectives  61.4 us (28%)
  local copies, waits for them, and re-layouts  27.2 us (12%)
  other arithmetic  23.1 us (10%)
  matrix products  17.4 us (8%)
  between operations  14.2 us (6%)
    all_gather x1, waiting for transfers between devices, per_device(): new_weight = lax.all_gather(updated, 'shard', axis=1, tiled=True)  75.9 us
    all_to_all x2, blocking collectives, copy_for_each(): return lax.all_to_all(copies, axis, split_axis=0, concat_axis=0, tiled=True)  28.6 us
    all_to_all x1, blocking collectives, sum_in_two_steps(): lax.all_to_all(nearer, far, split_axis=0, concat_axis=0, tiled=True)  24.6 us
    unnamed x4, other arithmetic  12.4 us
    all_to_all x1, blocking collectives, sent_and_summed(): blocks = lax.all_to_all(in_blocks(array, dim, size), axis, 0, 0, tiled=True)  8.23 us
    dot_general x2, matrix products, decode(): jnp.einsum('ai,xyab,bj->xiyj', basis_table, square, basis_table, precisio...  6.6 us
    mul x2, local copies, waits for them, and re-layouts, per_device(): step_rate * smooth  5.27 us
    dot_general x1, matrix products, expand(): jnp.einsum('xyki,xyk,xykj->xiyj', left_rows, values, right_rows, precisio...  5.07 us
  transfers between devices with their start and end apart: 1, of which 1 were waited for; matrix products, arithmetic and copies ran while one was open for 6% of the time, Pallas kernels for 0%

commit v1 on v0

--- a/solution.py
+++ b/solution.py
@@ -118,7 +118,8 @@
     summed = sum_by_parts(fill_grid(picked, own_pos), (("replica_0", "replica_1"), "replica_2"))
     smooth = jnp.tanh(decode(summed, basis_table))
     updated = (weight.astype(jnp.float32) - step_rate * smooth).astype(jnp.bfloat16)
-    new_weight = lax.all_gather(updated, "shard", axis=1, tiled=True)
+    outgoing = jnp.stack([updated] * lax.axis_size("shard"))
+    new_weight = jnp.concatenate(lax.all_to_all(outgoing, "shard", 0, 0), axis=1)
     direction = smooth.astype(jnp.bfloat16)
     return (kept_state[None], direction, new_weight)
 

time: 220 us -> 183 us (0.83)
  waiting for transfers between devices: 76 us -> 35.2 us
  between operations: 14.2 us -> 0.79 us
  local copies, waits for them, and re-layouts: 27.2 us -> 39.3 us
  starting transfers between devices: 0.04 us -> 5.51 us
    all_gather x1 -> x0, waiting for transfers between devices: 75.9 us -> none  [per_device(): new_weight = lax.all_gather(updated, 'shard', axis=1, tiled=True)]
    all_to_all x0 -> x1, waiting for transfers between devices: none -> 35.2 us  [per_device(): lax.all_to_all(outgoing, 'shard', 0, 0)]
    all_to_all x0 -> x1, local copies, waits for them, and re-layouts: none -> 6.45 us  [per_device(): lax.all_to_all(outgoing, 'shard', 0, 0)]
    all_to_all x0 -> x1, starting transfers between devices: none -> 5.51 us  [per_device(): lax.all_to_all(outgoing, 'shard', 0, 0)]
    another operation x0 -> x1, local copies, waits for them, and re-layouts: none -> 2.55 us  [per_device(): outgoing = jnp.stack([updated] * lax.axis_size('shard'))]
    unnamed x12 -> x8, local copies, waits for them, and re-layouts: 4.74 us -> 6.72 us
  transfers between devices with their start and end apart: 1 -> 1, of which waited for: 1 -> 1; matrix products, arithmetic and copies ran while one was open for 6% -> 7% of each run, Pallas kernels for 0% -> 0%
where the time goes in v1:
time: 183 us; the launch traced here: 182 us
  blocking collectives  61.4 us (34%)
  local copies, waits for them, and re-layouts  39.3 us (21%)
  waiting for transfers between devices  35.2 us (19%)
  other arithmetic  22.2 us (12%)
  matrix products  17.5 us (10%)
  starting transfers between devices  5.51 us (3%)
    all_to_all x1, waiting for transfers between devices, per_device(): lax.all_to_all(outgoing, 'shard', 0, 0)  35.2 us
    all_to_all x2, blocking collectives, copy_for_each(): return lax.all_to_all(copies, axis, split_axis=0, concat_axis=0, tiled=True)  28.6 us
    all_to_all x1, blocking collectives, sum_in_two_steps(): lax.all_to_all(nearer, far, split_axis=0, concat_axis=0, tiled=True)  24.6 us
    unnamed x4, other arithmetic  13.7 us
    all_to_all x1, blocking collectives, sent_and_summed(): blocks = lax.all_to_all(in_blocks(array, dim, size), axis, 0, 0, tiled=True)  8.23 us
    unnamed x8, local copies, waits for them, and re-layouts  6.72 us
    dot_general x2, matrix products, decode(): jnp.einsum('ai,xyab,bj->xiyj', basis_table, square, basis_table, precisio...  6.7 us
    all_to_all x1, local copies, waits for them, and re-layouts, per_device(): lax.all_to_all(outgoing, 'shard', 0, 0)  6.45 us
  transfers between devices with their start and end apart: 1, of which 1 were waited for; matrix products, arithmetic and copies ran while one was open for 7% of the time, Pallas kernels for 0%

profile of v1, /device:TPU:1, one launch (start us, length us, event | category | flops | bytes accessed | tf_op | source)
XLA Modules:
  0.0 181.9 jit_solution(1802421718927631392)
XLA Ops:
  0.6 0.8 compare_select_fusion
  1.4 0.8 add_select_fusion
  2.2 0.7 and_reduce_fusion
  3.0 0.7 multiply_reduce_fusion
  3.7 0.1 reshape.137
  3.8 0.0 copy-start.1
  3.8 0.0 copy-start.2
  3.8 0.8 fusion.11
  4.6 0.8 fusion.10
  5.4 0.0 copy-done.1
  5.4 0.0 copy-done.2
  5.4 0.1 convert_add_fusion
  5.6 1.9 %add.62 = f32[4,64,16,64]{3,2,1,0:T(8,128)} reshape(f32[1,256,1024]{2,1,0:T(8,128)S(1)} %convert_add_fusion) | data formatting | bytes 2097152 | tf_op jit(solution)/shard_map/add | solution.py:115
  7.4 4.2 %fusion.5 = f32[4,16,32]{2,1,0:T(8,128)S(1)} fusion(f32[4,16,32,64]{3,2,1,0:T(8,128)S(1)} %fusion.11, f32[4,16,32,64]{3,2,1,0:T(8,128)S(1)} %fusion.10, f32[4,64,16,64]{3,2,1,0:T(8,128)} %add.62), kind=kOutput, calls=%fused_computation.7 | convolution fusion | flops 100923392 | bytes 2105344 | tf_op jit(solution)/shard_map/xyki,xiyj->xykj/dot_general | solution.py:79
  11.6 0.1 reshape.139
  11.7 12.2 %scatter_custom_fusion = f32[262144]{0:T(1024)} fusion(s32[2048]{0:T(1024)S(1)} %reshape.137, f32[2048]{0:T(1024)S(1)} %reshape.139, f32[]{:T(128)} %constant.54.clone.1), kind=kCustom, calls=%fused_computation.16 | custom fusion | flops 2048 | bytes 1048580
  23.9 2.7 %reshape_reshape.3 = f32[16,2,2,4096]{3,2,1,0:T(2,128)} reshape(f32[262144]{0:T(1024)} %scatter_custom_fusion) | data formatting | bytes 2097152 | tf_op jit(solution)/shard_map/reshape;reshape | solution.py:38
  26.7 1.3 copy.41
  28.0 8.2 %all_to_all.25 = f32[2,16,2,4096]{3,2,1,0:T(2,128)} all-to-all(f32[2,16,2,4096]{3,2,1,0:T(2,128)S(1)} %copy.41), channel_id=1, replica_groups=mesh['replica_0'=4,'replica_1'=4,'replica_2'=2,'shard'=8] {'replica_2'}, dimensions={0} | all-to-all | bytes 2097152 | tf_op jit(solution)/shard_map/all_to_all | solution.py:43
  36.2 2.9 %reduce_sum.28 = f32[16,2,4096]{2,1,0:T(2,128)} reduce(f32[2,16,2,4096]{3,2,1,0:T(2,128)} %all_to_all.25, f32[]{:T(128)} %constant.54.clone.1), dimensions={0}, to_apply=%region_2.3 | reduce | flops 131072 | bytes 1572868 | tf_op jit(solution)/shard_map/reduce_sum | solution.py:44
  39.1 24.6 %all_to_all.26 = f32[16,2,4096]{2,1,0:T(2,128)} all-to-all(f32[16,2,4096]{2,1,0:T(2,128)} %reduce_sum.28), channel_id=1, replica_groups=mesh['replica_0'=4,'replica_1'=4,'replica_2'=2,'shard'=8] {'replica_0','..., dimensions={0} | all-to-all | bytes 1048576 | tf_op jit(solution)/shard_map/all_to_all | solution.py:51
  63.7 1.2 reduce_sum.29
  64.9 0.2 broadcast_in_dim.23
  65.1 20.8 %all_to_all.27 = f32[16,2,4096]{2,1,0:T(2,128)S(1)} all-to-all(f32[16,2,4096]{2,1,0:T(2,128)S(1)} %broadcast_in_dim.23), channel_id=1, replica_groups=mesh['replica_0'=4,'replica_1'=4,'replica_2'=2,'shard'=8] {'replica_0','..., dimensions={0} | all-to-all | bytes 1048576 | tf_op jit(solution)/shard_map/all_to_all | solution.py:21
  86.0 0.6 broadcast_in_dim.24
  86.6 7.7 %all_to_all.28 = f32[2,16,2,4096]{3,2,1,0:T(2,128)S(1)} all-to-all(f32[2,16,2,4096]{3,2,1,0:T(2,128)S(1)} %broadcast_in_dim.24), channel_id=1, replica_groups=mesh['replica_0'=4,'replica_1'=4,'replica_2'=2,'shard'=8] {'replica_2'}, dimensions={0} | all-to-all | bytes 2097152 | tf_op jit(solution)/shard_map/all_to_all | solution.py:21
  94.3 1.0 copy.43
  95.4 3.2 %reshape_reshape_reshape_reshape.3 = f32[4,16,64,64]{3,2,1,0:T(8,128)} reshape(f32[16,2,2,4096]{3,2,1,0:T(2,128)} %copy.43) | data formatting | bytes 2097152 | tf_op jit(solution)/shard_map/reshape;reshape;reshape;reshape | solution.py:105
  98.5 3.6 %fusion.19 = f32[4,16,64,64]{2,3,1,0:T(8,128)S(1)} fusion(f32[4,16,64,64]{3,2,1,0:T(8,128)} %reshape_reshape_reshape_reshape.3, f32[64]{0:T(128)S(1)} %get-tuple-element.17, f32[64]{0:T(128)S(1)} %get-tuple-element.16), kind=kOutput, calls=%fused_computation.32 | convolution fusion | flops 201338880 | bytes 2097664 | tf_op jit(solution)/shard_map/ai,xyab,bj->xiyj/dot_general | solution.py:106
  102.2 3.1 %multiply_bitcast_fusion = (f32[4,64,16,64]{3,1,2,0:T(8,128)S(1)}, bf16[4,64,16,64]{3,1,2,0:T(8,128)(2,1)}) fusion(f32[4,16,64,64]{2,3,1,0:T(8,128)S(1)} %fusion.19, f32[64]{0:T(128)S(1)} %get-tuple-element.17, f32[64]{0:T(128)S(1)} %get-tuple-element.16), kind=kOutput, calls=%fused_computation.3 | convolution fusion | flops 201863168 | bytes 2621952 | tf_op jit(solution)/shard_map/ai,xyab,bj->xiyj/dot_general | solution.py:106
  105.2 2.5 %copy.47 = f32[4,64,16,64]{3,2,1,0:T(8,128)} copy(f32[4,64,16,64]{3,1,2,0:T(8,128)S(1)} %get-tuple-element.12) | data formatting | bytes 2097152 | tf_op jit(solution)/shard_map/mul | solution.py:120
  107.8 2.7 %mul.124 = f32[256,1024]{1,0:T(8,128)} reshape(f32[4,64,16,64]{3,2,1,0:T(8,128)} %copy.47) | data formatting | bytes 2097152 | tf_op jit(solution)/shard_map/mul | solution.py:120
  110.5 1.5 subtract_convert_fusion
  112.0 2.6 %stack.2 = bf16[8,256,1024]{2,1,0:T(8,128)(2,1)} broadcast(bf16[256,1024]{1,0:T(8,128)(2,1)S(1)} %subtract_convert_fusion), dimensions={1,2} | broadcast | bytes 4718592 | tf_op jit(solution)/shard_map/stack | solution.py:121
  114.6 5.5 %all-to-all-start.4 = ((bf16[8,256,1024]{2,1,0:T(8,128)(2,1)}), bf16[8,256,1024]{2,1,0:T(8,128)(2,1)}, u32[]{:S(2)}, u32[]{:S(2)}) async-start(bf16[8,256,1024]{2,1,0:T(8,128)(2,1)} %stack.2), calls=%async_computation.4 | async-start | bytes 8388608 | tf_op jit(solution)/shard_map/all_to_all | solution.py:122
  120.1 5.1 %convolution_bitcast_fusion = f32[4,64,16,64]{1,3,2,0:T(8,128)} fusion(f32[4,16,32,64]{3,2,1,0:T(8,128)S(1)} %fusion.10, f32[4,16,32,64]{3,2,1,0:T(8,128)S(1)} %fusion.11, f32[4,16,32]{2,1,0:T(8,128)S(1)} %fusion.5), kind=kOutput, calls=%fused_computation.5 | convolution fusion | flops 100794368 | bytes 2105344 | tf_op jit(solution)/shard_map/xyki,xyk,xykj->xiyj/dot_general | solution.py:89
  125.2 3.1 %copy.40 = f32[4,64,16,64]{3,2,1,0:T(8,128)} copy(f32[4,64,16,64]{1,3,2,0:T(8,128)} %convolution_bitcast_fusion) | data formatting | bytes 2097152 | tf_op jit(solution)/shard_map/xyki,xyk,xykj->xiyj/transpose | solution.py:89
  128.2 2.0 %reshape.129 = f32[1,256,1024]{2,1,0:T(8,128)S(1)} reshape(f32[4,64,16,64]{3,2,1,0:T(8,128)} %copy.40) | data formatting | bytes 2097152 | tf_op jit(solution)/shard_map/reshape | solution.py:92
  130.3 0.0 copy-start
  130.3 1.2 sub.16
  131.4 0.3 copy-done
  131.7 0.7 copy.46
  132.4 1.5 convert_element_type.28
  133.9 35.2 %all-to-all-done.4 = bf16[8,256,1024]{2,1,0:T(8,128)(2,1)} async-done(((bf16[8,256,1024]{2,1,0:T(8,128)(2,1)}), bf16[8,256,1024]{2,1,0:T(8,128)(2,1)}, u32[]{:S(2)}, u32[]{:S(2)}) %all-to-all-start.4) | async-done | bytes 4194336 | tf_op jit(solution)/shard_map/all_to_all | solution.py:122
  169.1 6.4 %copy.48 = bf16[8,256,1024]{1,2,0:T(8,128)(2,1)} copy(bf16[8,256,1024]{2,1,0:T(8,128)(2,1)} %all-to-all-done.4) | data formatting | bytes 8388608 | tf_op jit(solution)/shard_map/all_to_all | solution.py:122
  175.6 6.3 %copy.49 = bf16[256,8192]{1,0:T(8,128)(2,1)} copy(bf16[256,8192]{0,1:T(8,128)(2,1)} %bitcast.62) | data formatting | bytes 8388608
  (4 shorter events, 0.0 us)
Async XLA Ops:
  3.8 1.6 copy-start.1
  3.8 1.6 copy-start.2
  114.6 54.6 %all-to-all-start.4 = ((bf16[8,256,1024]{2,1,0:T(8,128)(2,1)}), bf16[8,256,1024]{2,1,0:T(8,128)(2,1)}, u32[]{:S(2)}, u32[]{:S(2)}) async-start(bf16[8,256,1024]{2,1,0:T(8,128)(2,1)} %stack.2), calls=%async_computation.4 | async-start | bytes 8388608 | tf_op jit(solution)/shard_map/all_to_all | solution.py:122
  130.3 1.5 copy-start
